TPU v7x, 32 devices: a whole 2x2x4 slice. The times are simulated.
32 devices in a mesh: fsdp: 8 (over y, x, core), seq: 4 (over z).
Axes of the slice: x: 2, y: 2, z: 4, core: 2. Of those that a mesh axis runs over, the one named last changes fastest.
Arguments:
- block_in: bfloat16 [20480, 640], P(('fsdp', 'seq')), may hold values from -134 to 134
- query_weight: bfloat16 [640, 1024], P('fsdp'), may hold values from -0.25 to 0.25
- key_weight: bfloat16 [640, 256], P('fsdp'), may hold values from -0.25 to 0.25
- value_weight: bfloat16 [640, 256], P('fsdp'), may hold values from -0.25 to 0.25
- output_weight: bfloat16 [1024, 640], P('fsdp'), may hold values from -0.1875 to 0.1875
- gate_weight: bfloat16 [640, 2048], P('fsdp'), may hold values from -0.25 to 0.25
- up_weight: bfloat16 [640, 2048], P('fsdp'), may hold values from -0.25 to 0.25
- down_weight: bfloat16 [2048, 640], P('fsdp'), may hold values from -0.125 to 0.125
- attention_norm: bfloat16 [640], P('fsdp'), may hold values from 0.099609375 to 1.8984375
- query_norm: bfloat16 [256], P('fsdp'), may hold values from 0.099609375 to 1.8984375
- key_norm: bfloat16 [256], P('fsdp'), may hold values from 0.099609375 to 1.8984375
- post_attention_norm: bfloat16 [640], P('fsdp'), may hold values from 0.099609375 to 1.8984375
- feedforward_norm: bfloat16 [640], P('fsdp'), may hold values from 0.099609375 to 1.8984375
- post_feedforward_norm: bfloat16 [640], P('fsdp'), may hold values from 0.099609375 to 1.8984375
- grad_out: bfloat16 [20480, 640], P(('fsdp', 'seq')), may hold values from -6 to 6
Outputs:
- block_out: bfloat16 [20480, 640], P(('fsdp', 'seq'))
- grad_in: bfloat16 [20480, 640], P(('fsdp', 'seq'))
- grad_query_weight: float32 [640, 1024], P('fsdp')
- grad_key_weight: float32 [640, 256], P('fsdp')
- grad_value_weight: float32 [640, 256], P('fsdp')
- grad_output_weight: float32 [1024, 640], P('fsdp')
- grad_gate_weight: float32 [640, 2048], P('fsdp')
- grad_up_weight: float32 [640, 2048], P('fsdp')
- grad_down_weight: float32 [2048, 640], P('fsdp')
- grad_attention_norm: float32 [640], P('fsdp')
- grad_query_norm: float32 [256], P('fsdp')
- grad_key_norm: float32 [256], P('fsdp')
- grad_post_attention_norm: float32 [640], P('fsdp')
- grad_feedforward_norm: float32 [640], P('fsdp')
- grad_post_feedforward_norm: float32 [640], P('fsdp')
All inputs are finite; a program needn't handle non-finite values.
Results may differ from a plain program's by a relative error of at most 0.018.
Values may be sent and summed in bfloat16 or wider, within the bound.
A program may use at most 128 MiB of HBM per device.

v0:
```python
import jax
import jax.numpy as jnp
from jax import lax
from jax.sharding import PartitionSpec as P

epsilon = 1e-06
rope_base = 1000000.0
negative = -1e30


def rms_scale(values, gain_row):
    return values * lax.rsqrt(jnp.mean(values * values, -1, keepdims=True) + epsilon) * gain_row


def rotate(values, cosine_table, sine_table):
    half_width = values.shape[-1] // 2
    first_half = values[..., :half_width]
    second = values[..., half_width:]
    return jnp.concatenate(
        [
            first_half * cosine_table - second * sine_table,
            second * cosine_table + first_half * sine_table,
        ],
        -1,
    )


def angles_for(positions, width):
    half_width = width // 2
    frequency = rope_base ** (-(jnp.arange(half_width).astype(jnp.float32) * 2.0 / width))
    angles = positions[:, None] * frequency[None, :]
    return (jnp.cos(angles), jnp.sin(angles))


def gelu_product(gate_lin, up_lin):
    return jax.nn.gelu(gate_lin, approximate=True) * up_lin


def rounded(values):
    return lax.optimization_barrier(values.astype(jnp.bfloat16)).astype(jnp.float32)


def masked_scores(query_rows, key_rows, first_pos, score_scale):
    block_rows = query_rows.shape[0]
    scores = (
        jnp.einsum("qhd,kd->hqk", query_rows, key_rows, preferred_element_type=jnp.float32)
        * score_scale
    )
    query_pos = first_pos + jnp.arange(block_rows, dtype=jnp.int32)
    key_pos = jnp.arange(key_rows.shape[0], dtype=jnp.int32)
    allowed = key_pos[None, :] <= query_pos[:, None]
    return jnp.where(allowed[None], scores, negative)


def attend_forward(queries, key_rows, value_rows, block_rows, query_offset):
    score_scale = queries.shape[-1] ** (-0.5)

    def one_block(block_index):
        row_start = block_index * block_rows
        query_rows = lax.dynamic_slice_in_dim(queries, row_start, block_rows, 0)
        scores = masked_scores(query_rows, key_rows, query_offset + row_start, score_scale)
        row_max = jnp.max(scores, -1, keepdims=True)
        exp_scores = jnp.exp(scores - row_max)
        row_total = jnp.sum(exp_scores, -1, keepdims=True)
        weights_low = (exp_scores / row_total).astype(jnp.bfloat16)
        block_out = jnp.einsum(
            "hqk,kd->qhd", weights_low, value_rows, preferred_element_type=jnp.float32
        )
        return (block_out, (row_max + jnp.log(row_total))[..., 0])

    outputs, log_totals = lax.map(
        one_block, jnp.arange(queries.shape[0] // block_rows, dtype=jnp.int32)
    )
    return (outputs.reshape(queries.shape), log_totals)


def attend_backward(queries, key_rows, value_rows, grad_rows, log_totals, block_rows, query_offset):
    score_scale = queries.shape[-1] ** (-0.5)

    def one_block(running, block_index):
        key_grad, value_grad = running
        row_start = block_index * block_rows
        query_rows = lax.dynamic_slice_in_dim(queries, row_start, block_rows, 0)
        grad_block = lax.dynamic_slice_in_dim(grad_rows, row_start, block_rows, 0)
        scores = masked_scores(query_rows, key_rows, query_offset + row_start, score_scale)
        weights = jnp.exp(scores - log_totals[block_index][..., None])
        grad_weights = jnp.einsum(
            "qhd,kd->hqk", grad_block, value_rows, preferred_element_type=jnp.float32
        )
        inner = jnp.sum(weights * grad_weights, -1, keepdims=True)
        grad_scores = (weights * (grad_weights - inner)).astype(jnp.bfloat16)
        query_grad = (
            jnp.einsum("hqk,kd->qhd", grad_scores, key_rows, preferred_element_type=jnp.float32)
            * score_scale
        )
        key_grad = (
            key_grad
            + jnp.einsum("hqk,qhd->kd", grad_scores, query_rows, preferred_element_type=jnp.float32)
            * score_scale
        )
        value_grad = value_grad + jnp.einsum(
            "hqk,qhd->kd",
            weights.astype(jnp.bfloat16),
            grad_block,
            preferred_element_type=jnp.float32,
        )
        return ((key_grad, value_grad), query_grad)

    zeros_rows = jnp.zeros(key_rows.shape, jnp.float32)
    (key_grad, value_grad), query_grads = lax.scan(
        one_block,
        (zeros_rows, zeros_rows),
        jnp.arange(queries.shape[0] // block_rows, dtype=jnp.int32),
    )
    return (query_grads.reshape(queries.shape), key_grad, value_grad)


def per_device(
    block_in,
    query_weight,
    key_weight,
    value_weight,
    output_weight,
    gate_weight,
    up_weight,
    down_weight,
    attention_norm,
    query_norm,
    key_norm,
    post_attention_norm,
    feedforward_norm,
    post_feedforward_norm,
    grad_out,
):
    gathered = (
        lax.all_gather(query_weight, "fsdp", axis=0, tiled=True),
        lax.all_gather(key_weight, "fsdp", axis=0, tiled=True),
        lax.all_gather(value_weight, "fsdp", axis=0, tiled=True),
        lax.all_gather(output_weight, "fsdp", axis=0, tiled=True),
        lax.all_gather(gate_weight, "fsdp", axis=0, tiled=True),
        lax.all_gather(up_weight, "fsdp", axis=0, tiled=True),
        lax.all_gather(down_weight, "fsdp", axis=0, tiled=True),
        lax.all_gather(attention_norm, "fsdp", axis=0, tiled=True),
        lax.all_gather(query_norm, "fsdp", axis=0, tiled=True),
        lax.all_gather(key_norm, "fsdp", axis=0, tiled=True),
        lax.all_gather(post_attention_norm, "fsdp", axis=0, tiled=True),
        lax.all_gather(feedforward_norm, "fsdp", axis=0, tiled=True),
        lax.all_gather(post_feedforward_norm, "fsdp", axis=0, tiled=True),
    )
    query_full, key_full, value_full, output_full, gate_full, up_full, down_full = gathered[:7]
    norm_gains = tuple((gain_row.astype(jnp.float32) for gain_row in gathered[7:]))
    attention_gain, query_gain, key_gain, post_attention_gain, second_gain, post_second_gain = (
        norm_gains
    )
    token_count = block_in.shape[0]
    head_size = query_gain.shape[0]
    head_count = query_full.shape[1] // head_size
    length = token_count * lax.axis_size("seq")
    block_rows = min(512, length)
    token_offset = lax.axis_index("seq") * token_count
    input_f = block_in.astype(jnp.float32)
    normed, pull_normed = jax.vjp(rms_scale, input_f, attention_gain)
    normed_low = normed.astype(jnp.bfloat16)
    query_lin = jnp.dot(normed_low, query_full, preferred_element_type=jnp.float32).reshape(
        token_count, head_count, head_size
    )
    key_lin = jnp.dot(normed_low, key_full, preferred_element_type=jnp.float32)
    value_low = jnp.dot(normed_low, value_full, preferred_element_type=jnp.float32).astype(
        jnp.bfloat16
    )
    positions = (token_offset + jnp.arange(token_count, dtype=jnp.int32)).astype(jnp.float32)
    cosine_table, sine_table = angles_for(positions, head_size)

    def query_piece(values, gain_row):
        return rotate(rms_scale(values, gain_row), cosine_table[:, None, :], sine_table[:, None, :])

    def key_piece(values, gain_row):
        return rotate(rms_scale(values, gain_row), cosine_table, sine_table)

    queries, pull_queries = jax.vjp(query_piece, query_lin, query_gain)
    key_rows, pull_keys = jax.vjp(key_piece, key_lin, key_gain)
    queries_low = queries.astype(jnp.bfloat16)
    key_all, value_all = (
        lax.all_gather(key_rows.astype(jnp.bfloat16), "seq", axis=0, tiled=True),
        lax.all_gather(value_low, "seq", axis=0, tiled=True),
    )
    query_heads = lax.all_to_all(queries_low, "seq", split_axis=1, concat_axis=0, tiled=True)
    head_out, log_totals = attend_forward(query_heads, key_all, value_all, block_rows, 0)
    mixed = lax.all_to_all(
        head_out.astype(jnp.bfloat16), "seq", split_axis=0, concat_axis=1, tiled=True
    ).reshape(token_count, head_count * head_size)
    attended = jnp.dot(mixed, output_full, preferred_element_type=jnp.float32)
    post_branch, pull_post = jax.vjp(rms_scale, attended, post_attention_gain)
    residual = input_f + post_branch
    normed_second, pull_second = jax.vjp(rms_scale, residual, second_gain)
    second_low = normed_second.astype(jnp.bfloat16)
    gate_lin = jnp.dot(second_low, gate_full, preferred_element_type=jnp.float32)
    up_lin = jnp.dot(second_low, up_full, preferred_element_type=jnp.float32)
    activated, pull_activated = jax.vjp(gelu_product, gate_lin, up_lin)
    activated_low = activated.astype(jnp.bfloat16)
    down_lin = jnp.dot(activated_low, down_full, preferred_element_type=jnp.float32)
    tail_branch, pull_tail = jax.vjp(rms_scale, down_lin, post_second_gain)
    block_out = (residual + tail_branch).astype(jnp.bfloat16)
    weights_back = (
        lax.all_gather(query_weight, "fsdp", axis=0, tiled=True),
        lax.all_gather(key_weight, "fsdp", axis=0, tiled=True),
        lax.all_gather(value_weight, "fsdp", axis=0, tiled=True),
        lax.all_gather(output_weight, "fsdp", axis=0, tiled=True),
        lax.all_gather(gate_weight, "fsdp", axis=0, tiled=True),
        lax.all_gather(up_weight, "fsdp", axis=0, tiled=True),
        lax.all_gather(down_weight, "fsdp", axis=0, tiled=True),
    )
    query_back, key_back, value_back, output_back, gate_back, up_back, down_back = weights_back
    grad_f = grad_out.astype(jnp.float32)
    grad_down, grad_post_second = pull_tail(grad_f)
    grad_down_low = grad_down.astype(jnp.bfloat16)
    grad_down_weight = jnp.einsum(
        "tf,td->fd", activated_low, grad_down_low, preferred_element_type=jnp.float32
    )
    grad_activated = jnp.einsum(
        "td,fd->tf", grad_down_low, down_back, preferred_element_type=jnp.float32
    )
    grad_gate, grad_up = pull_activated(grad_activated)
    gate_low = grad_gate.astype(jnp.bfloat16)
    up_low = grad_up.astype(jnp.bfloat16)
    grad_gate_weight = jnp.einsum(
        "td,tf->df", second_low, gate_low, preferred_element_type=jnp.float32
    )
    grad_up_weight = jnp.einsum("td,tf->df", second_low, up_low, preferred_element_type=jnp.float32)
    grad_second = jnp.einsum(
        "tf,df->td", gate_low, gate_back, preferred_element_type=jnp.float32
    ) + jnp.einsum("tf,df->td", up_low, up_back, preferred_element_type=jnp.float32)
    grad_resid_part, grad_second_gain = pull_second(grad_second)
    grad_residual = grad_f + grad_resid_part
    grad_attended, grad_post_attention = pull_post(grad_residual)
    attended_low = grad_attended.astype(jnp.bfloat16)
    grad_output_weight = jnp.einsum(
        "tq,td->qd", mixed, attended_low, preferred_element_type=jnp.float32
    )
    grad_mixed = (
        jnp.einsum("td,qd->tq", attended_low, output_back, preferred_element_type=jnp.float32)
        .astype(jnp.bfloat16)
        .reshape(token_count, head_count, head_size)
    )
    grad_head_rows = lax.all_to_all(grad_mixed, "seq", split_axis=1, concat_axis=0, tiled=True)
    query_head_grad, key_all_grad, value_all_grad = attend_backward(
        query_heads, key_all, value_all, grad_head_rows, log_totals, block_rows, 0
    )
    grad_queries = lax.all_to_all(
        query_head_grad.astype(jnp.bfloat16), "seq", split_axis=0, concat_axis=1, tiled=True
    )
    grad_keys, grad_values = (
        lax.psum_scatter(
            key_all_grad.astype(jnp.bfloat16), "seq", scatter_dimension=0, tiled=True
        ).astype(jnp.float32),
        lax.psum_scatter(
            value_all_grad.astype(jnp.bfloat16), "seq", scatter_dimension=0, tiled=True
        ).astype(jnp.float32),
    )
    grad_query_lin, grad_query_gain = pull_queries(grad_queries.astype(jnp.float32))
    grad_key_lin, grad_key_gain = pull_keys(rounded(grad_keys))
    query_lin_low = grad_query_lin.reshape(token_count, head_count * head_size).astype(jnp.bfloat16)
    key_lin_low = grad_key_lin.astype(jnp.bfloat16)
    value_lin_low = grad_values.astype(jnp.bfloat16)
    grad_query_weight = jnp.einsum(
        "td,tq->dq", normed_low, query_lin_low, preferred_element_type=jnp.float32
    )
    grad_key_weight = jnp.einsum(
        "td,tq->dq", normed_low, key_lin_low, preferred_element_type=jnp.float32
    )
    grad_value_weight = jnp.einsum(
        "td,tq->dq", normed_low, value_lin_low, preferred_element_type=jnp.float32
    )
    grad_normed = jnp.einsum(
        "tq,dq->td", query_lin_low, query_back, preferred_element_type=jnp.float32
    )
    grad_normed = grad_normed + jnp.einsum(
        "tq,dq->td", key_lin_low, key_back, preferred_element_type=jnp.float32
    )
    grad_normed = grad_normed + jnp.einsum(
        "tq,dq->td", value_lin_low, value_back, preferred_element_type=jnp.float32
    )
    grad_input_part, grad_attention_gain = pull_normed(grad_normed)
    grad_in = (grad_residual + grad_input_part).astype(jnp.bfloat16)
    scattered = (
        lax.psum_scatter(grad_query_weight, "fsdp", scatter_dimension=0, tiled=True),
        lax.psum_scatter(grad_key_weight, "fsdp", scatter_dimension=0, tiled=True),
        lax.psum_scatter(grad_value_weight, "fsdp", scatter_dimension=0, tiled=True),
        lax.psum_scatter(grad_output_weight, "fsdp", scatter_dimension=0, tiled=True),
        lax.psum_scatter(grad_gate_weight, "fsdp", scatter_dimension=0, tiled=True),
        lax.psum_scatter(grad_up_weight, "fsdp", scatter_dimension=0, tiled=True),
        lax.psum_scatter(grad_down_weight, "fsdp", scatter_dimension=0, tiled=True),
        lax.psum_scatter(grad_attention_gain, "fsdp", scatter_dimension=0, tiled=True),
        lax.psum_scatter(grad_query_gain, "fsdp", scatter_dimension=0, tiled=True),
        lax.psum_scatter(grad_key_gain, "fsdp", scatter_dimension=0, tiled=True),
        lax.psum_scatter(grad_post_attention, "fsdp", scatter_dimension=0, tiled=True),
        lax.psum_scatter(grad_second_gain, "fsdp", scatter_dimension=0, tiled=True),
        lax.psum_scatter(grad_post_second, "fsdp", scatter_dimension=0, tiled=True),
    )
    summed = (
        lax.psum(scattered[0].astype(jnp.bfloat16), "seq").astype(jnp.float32),
        lax.psum(scattered[1].astype(jnp.bfloat16), "seq").astype(jnp.float32),
        lax.psum(scattered[2].astype(jnp.bfloat16), "seq").astype(jnp.float32),
        lax.psum(scattered[3].astype(jnp.bfloat16), "seq").astype(jnp.float32),
        lax.psum(scattered[4].astype(jnp.bfloat16), "seq").astype(jnp.float32),
        lax.psum(scattered[5].astype(jnp.bfloat16), "seq").astype(jnp.float32),
        lax.psum(scattered[6].astype(jnp.bfloat16), "seq").astype(jnp.float32),
        lax.psum(scattered[7].astype(jnp.bfloat16), "seq").astype(jnp.float32),
        lax.psum(scattered[8].astype(jnp.bfloat16), "seq").astype(jnp.float32),
        lax.psum(scattered[9].astype(jnp.bfloat16), "seq").astype(jnp.float32),
        lax.psum(scattered[10].astype(jnp.bfloat16), "seq").astype(jnp.float32),
        lax.psum(scattered[11].astype(jnp.bfloat16), "seq").astype(jnp.float32),
        lax.psum(scattered[12].astype(jnp.bfloat16), "seq").astype(jnp.float32),
    )
    return (
        block_out,
        grad_in,
        summed[0],
        summed[1],
        summed[2],
        summed[3],
        summed[4],
        summed[5],
        summed[6],
        summed[7],
        summed[8],
        summed[9],
        summed[10],
        summed[11],
        summed[12],
    )


def solution(mesh):
    in_specs = (
        P(("fsdp", "seq"), None),
        P("fsdp", None),
        P("fsdp", None),
        P("fsdp", None),
        P("fsdp", None),
        P("fsdp", None),
        P("fsdp", None),
        P("fsdp", None),
        P("fsdp"),
        P("fsdp"),
        P("fsdp"),
        P("fsdp"),
        P("fsdp"),
        P("fsdp"),
        P(("fsdp", "seq"), None),
    )
    out_specs = (
        P(("fsdp", "seq"), None),
        P(("fsdp", "seq"), None),
        P("fsdp", None),
        P("fsdp", None),
        P("fsdp", None),
        P("fsdp", None),
        P("fsdp", None),
        P("fsdp", None),
        P("fsdp", None),
        P("fsdp"),
        P("fsdp"),
        P("fsdp"),
        P("fsdp"),
        P("fsdp"),
        P("fsdp"),
    )
    return jax.shard_map(
        per_device, mesh=mesh, in_specs=in_specs, out_specs=out_specs, check_vma=False
    )
```

profile of v0, /device:TPU:0, one launch (start us, length us, event | category | flops | bytes accessed | tf_op | source)
XLA Modules:
  0.0 985.4 jit_solution(9208684761553230560)
XLA Ops:
  14.0 15.8 %all-reduce.17 = (bf16[640]{0:T(1024)(128)(2,1)S(1)}, bf16[256]{0:T(256)(128)(2,1)S(1)}, bf16[256]{0:T(256)(128)(2,1)S(1)}, bf16[640]{0:T(1024)(128)(2,1)S(1)}, ...) all-reduce(bf16[640]{0:T(1024)(128)(2,1)S(1)} %dynamic-update-slice, ...), channel_id=1, replica_groups=mesh['fsdp'=8,'seq'=4] {'fsdp'}, use_global_device_ids=true, to_apply=%add.4 | all-reduce | flops 3072 | bytes 12288
  29.8 8.8 all_gather.55
  43.4 9.5 all_gather.58
  70.6 4.8 all-to-all-start
  78.5 49.1 %all-gather.12.cloned.1.call-done = bf16[2560,256]{1,0:T(8,128)(2,1)} async-done(((bf16[640,256]{1,0:T(8,128)(2,1)}), bf16[2560,256]{1,0:T(8,128)(2,1)}) %all-gather.12.cloned.1.call-update) | async-done | bytes 1310736 | tf_op jit(solution)/shard_map/all_gather | solution.py:185
  128.5 35.3 %while.27 = (s32[]{:T(128)}, bf16[5,512,1,256]{3,1,2,0:T(8,128)(2,1)S(1)}, f32[5,1,512]{2,1,0:T(1,128)S(1)}, s32[5]{0:T(128)S(1)}, bf16[2560,1,256]{2,0,1:T(8,12...) while((s32[]{:T(128)}, ...), condition=%wide.region_6.7_spmd, body=%wide.region_3.6_spmd.sunk | while | flops 1353973760 | bytes 19161280 | solution.py:71
  173.9 28.6 %all-to-all-done.1 = bf16[4,2,81920]{2,1,0:T(2,128)(2,1)S(1)} async-done(((bf16[4,2,81920]{2,1,0:T(2,128)(2,1)}), bf16[4,2,81920]{2,1,0:T(2,128)(2,1)S(1)}, u32[]{:S(2)}, u32[]{:S(2)}) %all-to-all-start.1) | async-done | bytes 1310752 | tf_op jit(solution)/shard_map/all_to_all | solution.py:189
  214.0 6.6 fusion.94
  220.6 10.1 %multiply_convert_fusion.1 = (bf16[640,2048]{1,0:T(8,128)(2,1)}, f32[640,2048]{1,0:T(8,128)}) fusion(f32[640,2048]{1,0:T(8,128)} %fusion.94, bf16[640,640]{0,1:T(8,128)(2,1)} %multiply_convert_fusion.2, bf16[640,2048]{1,0:T(8,128)(2,1)} %all-gather.18.cloned.1.call-done), kind=kOutput, calls=%fused_computation.58 | convolution fusion | flops 1690828800 | bytes 16547840 | tf_op jit(solution)/shard_map/dot_general | solution.py:198
  230.7 18.3 %all-gather.20.cloned.1.call-done = bf16[2048,640]{1,0:T(8,128)(2,1)} async-done(((bf16[256,640]{1,0:T(8,128)(2,1)}), bf16[2048,640]{1,0:T(8,128)(2,1)}) %all-gather.20.cloned.1.call-update) | async-done | bytes 2621456 | tf_op jit(solution)/shard_map/all_gather | solution.py:142
  249.0 5.0 multiply_reduce_fusion.6
  258.6 6.7 multiply_convert_fusion
  276.8 4.6 all-to-all-start.2
  281.4 31.9 %all-to-all-done.2 = bf16[640,4,256]{2,0,1:T(8,128)(2,1)} async-done(((bf16[640,4,256]{2,0,1:T(8,128)(2,1)}), bf16[640,4,256]{2,0,1:T(8,128)(2,1)}, u32[]{:S(2)}, u32[]{:S(2)}) %all-to-all-start.2) | async-done | bytes 1310752 | tf_op jit(solution)/shard_map/all_to_all | solution.py:245
  314.4 135.8 %while.28 = (s32[]{:T(128)}, f32[2560,256]{1,0:T(8,128)}, f32[2560,256]{1,0:T(8,128)}, bf16[5,512,1,256]{3,1,2,0:T(8,128)(2,1)}, s32[5]{0:T(128)S(1)}, /*index=5...) while((s32[]{:T(128)}, f32[2560,256]{1,0:T(8,128)}, ...), condition=%wide.region_15.16_spmd.clone, body=%wide.region_13.15_spmd.clone.sunk | while | flops 3371958272 | bytes 133970368 | solution.py:110
  315.8 4.7 fusion.180
  322.5 5.0 fusion.181
  337.4 3.8 fusion.184
  342.5 4.7 fusion.180
  349.2 5.0 fusion.181
  356.6 4.4 fusion.183
  364.7 3.8 fusion.184
  369.7 4.7 fusion.180
  376.4 5.0 fusion.181
  383.8 4.4 fusion.183
  391.9 3.8 fusion.184
  397.0 4.7 fusion.180
  403.7 5.0 fusion.181
  411.0 4.4 fusion.183
  419.2 3.8 fusion.184
  424.2 4.7 fusion.180
  430.9 5.0 fusion.181
  438.3 4.4 fusion.183
  446.4 3.8 fusion.184
  457.0 28.1 %reduce-scatter.28.cloned.1.call-done = bf16[640,256]{1,0:T(8,128)(2,1)} async-done(((bf16[2560,256]{1,0:T(8,128)(2,1)}), bf16[640,256]{1,0:T(8,128)(2,1)}) %reduce-scatter.28.cloned.1.call-update) | async-done | bytes 327696
  490.4 27.1 %reduce-scatter.12.cloned.1.call-done = bf16[640,256]{1,0:T(8,128)(2,1)} async-done(((bf16[2560,256]{1,0:T(8,128)(2,1)}), bf16[640,256]{1,0:T(8,128)(2,1)}) %reduce-scatter.12.cloned.1.call-update) | async-done | bytes 327696 | tf_op jit(solution)/shard_map/reduce_scatter | solution.py:256
  526.1 34.8 %all_to_all.60 = bf16[4,2,81920]{2,1,0:T(2,128)(2,1)} all-to-all(bf16[4,2,81920]{2,1,0:T(2,128)(2,1)S(1)} %reshape.445), channel_id=1, replica_groups=mesh['fsdp'=8,'seq'=4] {'seq'}, dimensions={0} | all-to-all | bytes 2621440 | tf_op jit(solution)/shard_map/all_to_all | solution.py:249
  573.5 6.3 fusion.98
  579.9 6.3 fusion.99
  587.4 6.6 fusion.100
  599.8 23.3 %all-reduce.16 = (bf16[640]{0:T(1024)(128)(2,1)S(1)}, bf16[256]{0:T(256)(128)(2,1)S(1)}, bf16[256]{0:T(256)(128)(2,1)S(1)}, bf16[640]{0:T(1024)(128)(2,1)S(1)}, ...) all-reduce(f32[640]{0:T(1024)S(1)} %get-tuple-element.377, ...), channel_id=11, replica_groups=mesh['fsdp'=8,'seq'=4] {'fsdp'}, use_global_device_ids=true, to_apply=%region_36.37.clone | all-reduce | flops 3072 | bytes 18432
  629.7 9.9 %reduce-scatter.20.cloned.1.call-done = f32[128,640]{1,0:T(8,128)} async-done(((f32[1024,640]{1,0:T(8,128)}), f32[128,640]{1,0:T(8,128)}) %reduce-scatter.20.cloned.1.call-update) | async-done | bytes 327696 | tf_op jit(solution)/shard_map/reduce_scatter | solution.py:289
  641.3 45.4 %reduce-scatter.14.cloned.1.call-done = f32[80,1024]{1,0:T(8,128)} async-done(((f32[640,1024]{1,0:T(8,128)}), f32[80,1024]{1,0:T(8,128)}) %reduce-scatter.14.cloned.1.call-update) | async-done | bytes 327696 | tf_op jit(solution)/shard_map/reduce_scatter | solution.py:286
  688.3 58.2 %reduce-scatter.22.cloned.1.call-done = f32[80,2048]{1,0:T(8,128)} async-done(((f32[640,2048]{1,0:T(8,128)}), f32[80,2048]{1,0:T(8,128)}) %reduce-scatter.22.cloned.1.call-update) | async-done | bytes 655376 | tf_op jit(solution)/shard_map/reduce_scatter | solution.py:290
  748.3 58.3 %reduce-scatter.24.cloned.1.call-done = f32[80,2048]{1,0:T(8,128)} async-done(((f32[640,2048]{1,0:T(8,128)}), f32[80,2048]{1,0:T(8,128)}) %reduce-scatter.24.cloned.1.call-update) | async-done | bytes 655376 | tf_op jit(solution)/shard_map/reduce_scatter | solution.py:291
  808.5 58.0 %reduce-scatter.26.cloned.1.call-done = f32[256,640]{1,0:T(8,128)} async-done(((f32[2048,640]{1,0:T(8,128)}), f32[256,640]{1,0:T(8,128)}) %reduce-scatter.26.cloned.1.call-update) | async-done | bytes 655376 | tf_op jit(solution)/shard_map/reduce_scatter | solution.py:292
  873.2 32.1 %all-reduce.23.cloned.1.call-done = (bf16[80,256]{1,0:T(8,128)(2,1)}, bf16[80,256]{1,0:T(8,128)(2,1)}, bf16[80]{0:T(256)(128)(2,1)}, bf16[32]{0:T(256)(128)(2,1)...) async-done(((bf16[80,256]{1,0:T(8,128)(2,1)}, bf16[80,256]{1,0:T(8,128)(2,1)}, bf16[80]{0:T(256)(128)(2,1)}, ...) | async-done | bytes 82704 | tf_op jit(solution)/shard_map/psum | solution.py:302
  915.0 56.3 %all-reduce.25.cloned.1.call-done = (bf16[80,1024]{1,0:T(8,128)(2,1)}, bf16[128,640]{1,0:T(8,128)(2,1)}, bf16[80,2048]{1,0:T(8,128)(2,1)}, bf16[80,2048]{1,0:T(8,128)(2,1)}, bf16[256,640]{1,0:T(8,128)(2,1)}) async-done(((bf16[80,1024]{1,0:T(8,128)(2,1)}, bf16[128,640]{1,0:T(8,128)(2,1)}, bf16[80,2048]{1,0:T(8,128)(2,1)}, bf16[80,2048]{1,0:T(8,128)(2,1)}, bf16[256,640]{1,0:T(8,128)(2,1)}), ...) | async-done | bytes 1310736 | tf_op jit(solution)/shard_map/psum | solution.py:301
  (439 shorter events, 214.4 us)
Async XLA Ops:
  7.2 5.3 copy-start.65
  7.2 5.6 copy-start.66
  7.2 5.8 copy-start.67
  7.2 6.1 copy-start.68
  7.2 6.3 copy-start.69
  7.2 6.5 copy-start.70
  7.2 22.6 %copy-start.42 = (bf16[80,256]{1,0:T(8,128)(2,1)S(1)}, bf16[80,256]{1,0:T(8,128)(2,1)}, u32[]{:S(2)}) copy-start(bf16[80,256]{1,0:T(8,128)(2,1)} %param.21) | copy-start | bytes 122884
  7.3 50.7 %all-gather.8.cloned.1.call-start = ((), (), s32[]{:S(2)}) async-start(), calls=%async_computation.13 | async-start | bytes 1474560 | tf_op jit(solution)/shard_map/all_gather | solution.py:136
  8.0 68.0 %all-gather.10.cloned.1.call-start = ((), (), s32[]{:S(2)}) async-start(), calls=%async_computation.14 | async-start | bytes 1638400 | tf_op jit(solution)/shard_map/all_gather | solution.py:184
  29.8 28.1 %copy-start.48 = (f32[640]{0:T(1024)}, f32[640]{0:T(1024)S(1)}, u32[]{:S(2)}) copy-start(f32[640]{0:T(1024)S(1)} %convert_element_type.223) | copy-start | bytes 7684
  29.8 10.3 %copy-start.55 = (f32[256]{0:T(256)}, f32[256]{0:T(256)S(1)}, u32[]{:S(2)}) copy-start(f32[256]{0:T(256)S(1)} %convert_element_type.228) | copy-start | bytes 3076
  39.5 18.4 %copy-start.50 = (f32[640]{0:T(1024)}, f32[640]{0:T(1024)S(1)}, u32[]{:S(2)}) copy-start(f32[640]{0:T(1024)S(1)} %fusion.76) | copy-start | bytes 7684
  43.3 84.3 %all-gather.12.cloned.1.call-start = ((), (), s32[]{:S(2)}) async-start(), calls=%async_computation.15 | async-start | bytes 1638400 | tf_op jit(solution)/shard_map/all_gather | solution.py:185
  54.9 153.8 %all-gather.14.cloned.1.call-start = ((), (), s32[]{:S(2)}) async-start(), calls=%async_computation.16 | async-start | bytes 1474560 | tf_op jit(solution)/shard_map/all_gather | solution.py:139
  55.5 158.5 %all-gather.16.cloned.1.call-start = ((), (), s32[]{:S(2)}) async-start(), calls=%async_computation.17 | async-start | bytes 2949120 | tf_op jit(solution)/shard_map/all_gather | solution.py:140
  56.1 11.2 %copy-start.57 = (f32[256]{0:T(256)}, f32[256]{0:T(256)S(1)}, u32[]{:S(2)}) copy-start(f32[256]{0:T(256)S(1)} %convert_element_type.225) | copy-start | bytes 3076
  60.6 6.8 copy-start.5
  70.6 57.8 %all-to-all-start = ((bf16[640,4,256]{2,0,1:T(8,128)(2,1)}), bf16[640,4,256]{2,0,1:T(8,128)(2,1)}, u32[]{:S(2)}, u32[]{:S(2)}) async-start(bf16[640,4,256]{2,0,1:T(8,128)(2,1)} %pad_maximum_fusion), calls=%async_computation | async-start | bytes 2621440 | tf_op jit(solution)/shard_map/all_to_all | solution.py:187
  75.4 145.2 %all-gather.18.cloned.1.call-start = ((), (), s32[]{:S(2)}) async-start(), calls=%async_computation.18 | async-start | bytes 2949120 | tf_op jit(solution)/shard_map/all_gather | solution.py:141
  167.7 34.8 %all-to-all-start.1 = ((bf16[4,2,81920]{2,1,0:T(2,128)(2,1)}), bf16[4,2,81920]{2,1,0:T(2,128)(2,1)S(1)}, u32[]{:S(2)}, u32[]{:S(2)}) async-start(bf16[4,2,81920]{2,1,0:T(2,128)(2,1)} %reshape.443), calls=%async_computation.1 | async-start | bytes 2621440 | tf_op jit(solution)/shard_map/all_to_all | solution.py:189
  171.2 77.8 %all-gather.20.cloned.1.call-start = ((), (), s32[]{:S(2)}) async-start(), calls=%async_computation.19 | async-start | bytes 2949120 | tf_op jit(solution)/shard_map/all_gather | solution.py:142
  249.0 7.8 copy-start.73
  256.9 8.4 copy-start.29
  258.5 6.7 copy-start.21
  276.8 36.5 %all-to-all-start.2 = ((bf16[640,4,256]{2,0,1:T(8,128)(2,1)}), bf16[640,4,256]{2,0,1:T(8,128)(2,1)}, u32[]{:S(2)}, u32[]{:S(2)}) async-start(bf16[640,4,256]{2,0,1:T(8,128)(2,1)} %bitcast.176), calls=%async_computation.2 | async-start | bytes 2621440 | tf_op jit(solution)/shard_map/all_to_all | solution.py:245
  281.4 203.7 %reduce-scatter.28.cloned.1.call-start = ((), (), s32[]{:S(2)}) async-start(), calls=%async_computation.28 | async-start | bytes 1638400
  322.5 5.1 slice-start
  403.6 5.1 slice-start
  455.6 61.9 %reduce-scatter.12.cloned.1.call-start = ((), (), s32[]{:S(2)}) async-start(), calls=%async_computation.20 | async-start | bytes 1638400 | tf_op jit(solution)/shard_map/reduce_scatter | solution.py:256
  456.9 29.4 %copy-start.45 = (f32[640]{0:T(1024)S(1)}, f32[640]{0:T(1024)}, u32[]{:S(2)}) copy-start(f32[640]{0:T(1024)} %copy-done.44) | copy-start | bytes 7684
  456.9 29.5 %copy-start.60 = (f32[128]{0:T(128)S(1)}, f32[128]{0:T(128)}, u32[]{:S(2)}) copy-start(f32[128]{0:T(128)} %copy-done.59) | copy-start | bytes 1540
  456.9 30.9 %copy-start.12 = (f32[640,256]{0,1:T(8,128)S(1)}, f32[640,256]{0,1:T(8,128)}, u32[]{:S(2)}) copy-start(f32[640,256]{0,1:T(8,128)} %copy-done.11) | copy-start | bytes 1966084
  456.9 30.9 %copy-start.41 = (f32[640]{0:T(1024)S(1)}, f32[640]{0:T(1024)}, u32[]{:S(2)}) copy-start(f32[640]{0:T(1024)} %copy-done.40) | copy-start | bytes 7684
  456.9 30.9 %copy-start.56 = (f32[256]{0:T(256)S(1)}, f32[256]{0:T(256)}, u32[]{:S(2)}) copy-start(f32[256]{0:T(256)} %copy-done.55) | copy-start | bytes 3076
  456.9 169.7 %reduce-scatter.16.cloned.1.call-start = ((), (), s32[]{:S(2)}) async-start(), calls=%async_computation.22 | async-start | bytes 737280 | tf_op jit(solution)/shard_map/reduce_scatter | solution.py:287
  490.3 29.5 %copy-start.28 = (bf16[640,4,1,256]{0,3,1,2:T(8,128)(2,1)S(1)}, bf16[640,4,1,256]{0,3,1,2:T(8,128)(2,1)}, u32[]{:S(2)}) copy-start(bf16[640,4,1,256]{0,3,1,2:T(8,128)(2,1)} %copy.171) | copy-start | bytes 3932164
  490.3 29.6 %copy-start.32 = (bf16[640,640]{0,1:T(8,128)(2,1)S(1)}, bf16[640,640]{0,1:T(8,128)(2,1)}, u32[]{:S(2)}) copy-start(bf16[640,640]{0,1:T(8,128)(2,1)} %copy-done.31) | copy-start | bytes 2457604
  490.3 137.8 %reduce-scatter.18.cloned.1.call-start = ((), (), s32[]{:S(2)}) async-start(), calls=%async_computation.23 | async-start | bytes 737280 | tf_op jit(solution)/shard_map/reduce_scatter | solution.py:288
  519.8 119.8 %reduce-scatter.20.cloned.1.call-start = ((), (), s32[]{:S(2)}) async-start(), calls=%async_computation.24 | async-start | bytes 2949120 | tf_op jit(solution)/shard_map/reduce_scatter | solution.py:289
  522.7 163.9 %reduce-scatter.14.cloned.1.call-start = ((), (), s32[]{:S(2)}) async-start(), calls=%async_computation.21 | async-start | bytes 2949120 | tf_op jit(solution)/shard_map/reduce_scatter | solution.py:286
  572.4 174.1 %reduce-scatter.22.cloned.1.call-start = ((), (), s32[]{:S(2)}) async-start(), calls=%async_computation.25 | async-start | bytes 5898240 | tf_op jit(solution)/shard_map/reduce_scatter | solution.py:290
  579.8 226.9 %reduce-scatter.24.cloned.1.call-start = ((), (), s32[]{:S(2)}) async-start(), calls=%async_computation.26 | async-start | bytes 5898240 | tf_op jit(solution)/shard_map/reduce_scatter | solution.py:291
  586.2 280.3 %reduce-scatter.26.cloned.1.call-start = ((), (), s32[]{:S(2)}) async-start(), calls=%async_computation.27 | async-start | bytes 5898240 | tf_op jit(solution)/shard_map/reduce_scatter | solution.py:292
  594.0 311.3 %all-reduce.23.cloned.1.call-start = ((), (), s32[]{:S(2)}) async-start(), calls=%async_computation.29 | async-start | bytes 169984 | tf_op jit(solution)/shard_map/psum | solution.py:302
  629.7 341.7 %all-reduce.25.cloned.1.call-start = ((), (), s32[]{:S(2)}) async-start(), calls=%async_computation.30 | async-start | bytes 2621440 | tf_op jit(solution)/shard_map/psum | solution.py:301
  748.3 120.1 %copy-start.15 = (bf16[640,640]{0,1:T(8,128)(2,1)S(1)}, bf16[640,640]{0,1:T(8,128)(2,1)}, u32[]{:S(2)}) copy-start(bf16[640,640]{0,1:T(8,128)(2,1)} %get-tuple-element.454) | copy-start | bytes 2457604
  971.3 5.3 copy-start.35
  971.3 6.1 copy-start.34
  (73 other events, 186.8 us)
Sparse Core Ops, SparseCore 0:
  10.0 28.3 all-gather.7
  43.4 32.5 all-gather.9
  78.2 49.3 all-gather.11
  129.3 23.8 all-gather.13
  154.9 30.1 all-gather.15
  186.8 30.1 all-gather.17
  218.9 30.1 all-gather.19
  455.7 29.3 reduce-scatter.27
  487.4 30.0 reduce-scatter.11
  521.0 33.3 reduce-scatter.15
  558.1 34.5 reduce-scatter.17
  595.9 43.6 reduce-scatter.19
  643.0 43.6 reduce-scatter.13
  689.9 56.5 reduce-scatter.21
  750.1 56.5 reduce-scatter.23
  809.9 56.5 reduce-scatter.25
  870.7 34.6 all-reduce.22
  909.1 62.2 all-reduce.24
where the time goes:
time: 996 us; the launch traced here: 985 us
  waiting for transfers between devices  505 us (51%)
  matrix products  203 us (20%)
  blocking collectives  92.3 us (9%)
  local copies, waits for them, and re-layouts  76 us (8%)
  other arithmetic  59.7 us (6%)
  between operations  18.2 us (2%)
  loops' own time  17.1 us (2%)
  starting transfers between devices  13.8 us (1%)
    reduce_scatter x1, waiting for transfers between devices, per_device(): lax.psum_scatter(grad_up_weight, 'fsdp', scatter_dimension=0, tiled=True)  58.3 us
    reduce_scatter x1, waiting for transfers between devices, per_device(): lax.psum_scatter(grad_gate_weight, 'fsdp', scatter_dimension=0, tiled=True)  58.2 us
    reduce_scatter x1, waiting for transfers between devices, per_device(): lax.psum_scatter(grad_down_weight, 'fsdp', scatter_dimension=0, tiled=True)  58 us
    psum x1, waiting for transfers between devices, per_device(): lax.psum(scattered[0].astype(jnp.bfloat16), 'seq').astype(jnp.float32)  56.3 us
    all_gather x1, waiting for transfers between devices, per_device(): lax.all_gather(value_low, 'seq', axis=0, tiled=True)  49.1 us
    reduce_scatter x1, waiting for transfers between devices, per_device(): lax.psum_scatter(grad_query_weight, 'fsdp', scatter_dimension=0, tiled=True)  45.4 us
    unnamed x170, local copies, waits for them, and re-layouts  42.3 us
    unnamed x2, blocking collectives  39.2 us
  transfers between devices with their start and end apart: 21, of which 15 were waited for; matrix products, arithmetic and copies ran while one was open for 17% of the time, Pallas kernels for 0%

commit v1 on v0

--- a/solution.py
+++ b/solution.py
@@ -2,10 +2,20 @@
 import jax.numpy as jnp
 from jax import lax
 from jax.sharding import PartitionSpec as P
+from jax.lax import all_to_all, axis_size
 
 epsilon = 1e-06
 rope_base = 1000000.0
 negative = -1e30
+
+
+def view_sector(x_part):
+    return jnp.concatenate(
+        all_to_all(
+            jnp.stack(jnp.split(x_part, axis_size("seq"), 1)), "seq", split_axis=0, concat_axis=0
+        ),
+        0,
+    )
 
 
 def rms_scale(values, gain_row):
@@ -242,7 +252,7 @@
         .astype(jnp.bfloat16)
         .reshape(token_count, head_count, head_size)
     )
-    grad_head_rows = lax.all_to_all(grad_mixed, "seq", split_axis=1, concat_axis=0, tiled=True)
+    grad_head_rows = view_sector(grad_mixed)
     query_head_grad, key_all_grad, value_all_grad = attend_backward(
         query_heads, key_all, value_all, grad_head_rows, log_totals, block_rows, 0
     )

time: 996 us -> 999 us (level)
  transfers between devices with their start and end apart: 21 -> 21, of which waited for: 15 -> 14; matrix products, arithmetic and copies ran while one was open for 17% -> 17% of each run, Pallas kernels for 0% -> 0%
where the time goes in v1:
time: 999 us; the launch traced here: 989 us
  waiting for transfers between devices  505 us (51%)
  matrix products  203 us (20%)
  blocking collectives  92.4 us (9%)
  local copies, waits for them, and re-layouts  78.2 us (8%)
  other arithmetic  61 us (6%)
  between operations  18.4 us (2%)
  loops' own time  17.1 us (2%)
  starting transfers between devices  14 us (1%)
    reduce_scatter x1, waiting for transfers between devices, per_device(): lax.psum_scatter(grad_up_weight, 'fsdp', scatter_dimension=0, tiled=True)  58.4 us
    reduce_scatter x1, waiting for transfers between devices, per_device(): lax.psum_scatter(grad_gate_weight, 'fsdp', scatter_dimension=0, tiled=True)  58.2 us
    reduce_scatter x1, waiting for transfers between devices, per_device(): lax.psum_scatter(grad_down_weight, 'fsdp', scatter_dimension=0, tiled=True)  58 us
    psum x1, waiting for transfers between devices, per_device(): lax.psum(scattered[0].astype(jnp.bfloat16), 'seq').astype(jnp.float32)  56.2 us
    all_gather x1, waiting for transfers between devices, per_device(): lax.all_gather(value_low, 'seq', axis=0, tiled=True)  49.1 us
    reduce_scatter x1, waiting for transfers between devices, per_device(): lax.psum_scatter(grad_query_weight, 'fsdp', scatter_dimension=0, tiled=True)  45.3 us
    unnamed x170, local copies, waits for them, and re-layouts  42.4 us
    unnamed x2, blocking collectives  39.2 us
  transfers between devices with their start and end apart: 21, of which 14 were waited for; matrix products, arithmetic and copies ran while one was open for 17% of the time, Pallas kernels for 0%

profile of v1, /device:TPU:0, one launch (start us, length us, event | category | flops | bytes accessed | tf_op | source)
XLA Modules:
  0.0 988.8 jit_solution(7116260009605679735)
XLA Ops:
  14.0 15.8 %all-reduce.17 = (bf16[640]{0:T(1024)(128)(2,1)S(1)}, bf16[256]{0:T(256)(128)(2,1)S(1)}, bf16[256]{0:T(256)(128)(2,1)S(1)}, bf16[640]{0:T(1024)(128)(2,1)S(1)}, ...) all-reduce(bf16[640]{0:T(1024)(128)(2,1)S(1)} %dynamic-update-slice, ...), channel_id=1, replica_groups=mesh['fsdp'=8,'seq'=4] {'fsdp'}, use_global_device_ids=true, to_apply=%add.4 | all-reduce | flops 3072 | bytes 12288
  29.8 8.8 all_gather.55
  43.4 9.5 all_gather.58
  70.6 4.8 all-to-all-start
  78.5 49.1 %all-gather.12.cloned.1.call-done = bf16[2560,256]{1,0:T(8,128)(2,1)} async-done(((bf16[640,256]{1,0:T(8,128)(2,1)}), bf16[2560,256]{1,0:T(8,128)(2,1)}) %all-gather.12.cloned.1.call-update) | async-done | bytes 1310736 | tf_op jit(solution)/shard_map/all_gather | solution.py:195
  128.5 35.3 %while.27 = (s32[]{:T(128)}, bf16[5,512,1,256]{3,1,2,0:T(8,128)(2,1)S(1)}, f32[5,1,512]{2,1,0:T(1,128)S(1)}, s32[5]{0:T(128)S(1)}, bf16[2560,1,256]{2,0,1:T(8,12...) while((s32[]{:T(128)}, ...), condition=%wide.region_6.7_spmd, body=%wide.region_3.6_spmd.sunk | while | flops 1353973760 | bytes 19161280 | solution.py:81
  173.9 28.6 %all-to-all-done.1 = bf16[4,2,81920]{2,1,0:T(2,128)(2,1)S(1)} async-done(((bf16[4,2,81920]{2,1,0:T(2,128)(2,1)}), bf16[4,2,81920]{2,1,0:T(2,128)(2,1)S(1)}, u32[]{:S(2)}, u32[]{:S(2)}) %all-to-all-start.1) | async-done | bytes 1310752 | tf_op jit(solution)/shard_map/all_to_all | solution.py:199
  214.0 6.6 fusion.95
  220.7 10.1 %multiply_convert_fusion.1 = (bf16[640,2048]{1,0:T(8,128)(2,1)}, f32[640,2048]{1,0:T(8,128)}) fusion(f32[640,2048]{1,0:T(8,128)} %fusion.95, bf16[640,640]{0,1:T(8,128)(2,1)} %multiply_convert_fusion.2, bf16[640,2048]{1,0:T(8,128)(2,1)} %all-gather.18.cloned.1.call-done), kind=kOutput, calls=%fused_computation.58 | convolution fusion | flops 1690828800 | bytes 16547840 | tf_op jit(solution)/shard_map/dot_general | solution.py:208
  230.7 18.3 %all-gather.20.cloned.1.call-done = bf16[2048,640]{1,0:T(8,128)(2,1)} async-done(((bf16[256,640]{1,0:T(8,128)(2,1)}), bf16[2048,640]{1,0:T(8,128)(2,1)}) %all-gather.20.cloned.1.call-update) | async-done | bytes 2621456 | tf_op jit(solution)/shard_map/all_gather | solution.py:152
  249.1 5.0 multiply_reduce_fusion.6
  258.6 6.4 multiply_convert_fusion
  280.0 4.6 all-to-all-start.2
  284.6 31.9 %all-to-all-done.2 = bf16[4,640,1,256]{3,1,2,0:T(8,128)(2,1)} async-done(((bf16[4,640,1,256]{3,1,2,0:T(8,128)(2,1)}), bf16[4,640,1,256]{3,1,2,0:T(8,128)(2,1)}, u32[]{:S(2)}, u32[]{:S(2)}) %all-to-all-start.2) | async-done | bytes 1310752 | tf_op jit(solution)/shard_map/all_to_all | solution.py:14
  317.7 135.8 %while.28 = (s32[]{:T(128)}, f32[2560,256]{1,0:T(8,128)}, f32[2560,256]{1,0:T(8,128)}, bf16[5,512,1,256]{3,1,2,0:T(8,128)(2,1)}, s32[5]{0:T(128)S(1)}, /*index=5...) while((s32[]{:T(128)}, f32[2560,256]{1,0:T(8,128)}, ...), condition=%wide.region_15.16_spmd.clone, body=%wide.region_13.15_spmd.clone.sunk | while | flops 3371958272 | bytes 133970368 | solution.py:120
  319.1 4.7 fusion.181
  325.8 5.0 fusion.182
  340.7 3.8 fusion.185
  345.8 4.7 fusion.181
  352.4 5.0 fusion.182
  359.8 4.4 fusion.184
  367.9 3.8 fusion.185
  373.0 4.7 fusion.181
  379.7 5.0 fusion.182
  387.0 4.4 fusion.184
  395.2 3.8 fusion.185
  400.2 4.7 fusion.181
  406.9 5.0 fusion.182
  414.3 4.4 fusion.184
  422.4 3.8 fusion.185
  427.4 4.7 fusion.181
  434.1 5.0 fusion.182
  441.5 4.4 fusion.184
  449.6 3.8 fusion.185
  460.2 28.1 %reduce-scatter.28.cloned.1.call-done = bf16[640,256]{1,0:T(8,128)(2,1)} async-done(((bf16[2560,256]{1,0:T(8,128)(2,1)}), bf16[640,256]{1,0:T(8,128)(2,1)}) %reduce-scatter.28.cloned.1.call-update) | async-done | bytes 327696
  493.6 27.1 %reduce-scatter.12.cloned.1.call-done = bf16[640,256]{1,0:T(8,128)(2,1)} async-done(((bf16[2560,256]{1,0:T(8,128)(2,1)}), bf16[640,256]{1,0:T(8,128)(2,1)}) %reduce-scatter.12.cloned.1.call-update) | async-done | bytes 327696 | tf_op jit(solution)/shard_map/reduce_scatter | solution.py:266
  529.3 34.9 %all_to_all.47 = bf16[4,2,81920]{2,1,0:T(2,128)(2,1)} all-to-all(bf16[4,2,81920]{2,1,0:T(2,128)(2,1)S(1)} %reshape.449), channel_id=1, replica_groups=mesh['fsdp'=8,'seq'=4] {'seq'}, dimensions={0} | all-to-all | bytes 2621440 | tf_op jit(solution)/shard_map/all_to_all | solution.py:259
  576.8 6.3 fusion.99
  583.1 6.3 fusion.100
  590.6 6.6 fusion.101
  603.0 23.4 %all-reduce.16 = (bf16[640]{0:T(1024)(128)(2,1)S(1)}, bf16[256]{0:T(256)(128)(2,1)S(1)}, bf16[256]{0:T(256)(128)(2,1)S(1)}, bf16[640]{0:T(1024)(128)(2,1)S(1)}, ...) all-reduce(f32[640]{0:T(1024)S(1)} %get-tuple-element.377, ...), channel_id=11, replica_groups=mesh['fsdp'=8,'seq'=4] {'fsdp'}, use_global_device_ids=true, to_apply=%region_36.37.clone | all-reduce | flops 3072 | bytes 18432
  633.0 9.7 reduce-scatter.20.cloned.1.call-done
  644.5 45.3 %reduce-scatter.14.cloned.1.call-done = f32[80,1024]{1,0:T(8,128)} async-done(((f32[640,1024]{1,0:T(8,128)}), f32[80,1024]{1,0:T(8,128)}) %reduce-scatter.14.cloned.1.call-update) | async-done | bytes 327696 | tf_op jit(solution)/shard_map/reduce_scatter | solution.py:296
  691.4 58.2 %reduce-scatter.22.cloned.1.call-done = f32[80,2048]{1,0:T(8,128)} async-done(((f32[640,2048]{1,0:T(8,128)}), f32[80,2048]{1,0:T(8,128)}) %reduce-scatter.22.cloned.1.call-update) | async-done | bytes 655376 | tf_op jit(solution)/shard_map/reduce_scatter | solution.py:300
  751.4 58.4 %reduce-scatter.24.cloned.1.call-done = f32[80,2048]{1,0:T(8,128)} async-done(((f32[640,2048]{1,0:T(8,128)}), f32[80,2048]{1,0:T(8,128)}) %reduce-scatter.24.cloned.1.call-update) | async-done | bytes 655376 | tf_op jit(solution)/shard_map/reduce_scatter | solution.py:301
  811.6 58.0 %reduce-scatter.26.cloned.1.call-done = f32[256,640]{1,0:T(8,128)} async-done(((f32[2048,640]{1,0:T(8,128)}), f32[256,640]{1,0:T(8,128)}) %reduce-scatter.26.cloned.1.call-update) | async-done | bytes 655376 | tf_op jit(solution)/shard_map/reduce_scatter | solution.py:302
  876.3 32.1 %all-reduce.23.cloned.1.call-done = (bf16[80,256]{1,0:T(8,128)(2,1)}, bf16[80,256]{1,0:T(8,128)(2,1)}, bf16[80]{0:T(256)(128)(2,1)}, bf16[32]{0:T(256)(128)(2,1)...) async-done(((bf16[80,256]{1,0:T(8,128)(2,1)}, bf16[80,256]{1,0:T(8,128)(2,1)}, bf16[80]{0:T(256)(128)(2,1)}, ...) | async-done | bytes 82704 | tf_op jit(solution)/shard_map/psum | solution.py:312
  918.3 56.2 %all-reduce.25.cloned.1.call-done = (bf16[80,1024]{1,0:T(8,128)(2,1)}, bf16[128,640]{1,0:T(8,128)(2,1)}, bf16[80,2048]{1,0:T(8,128)(2,1)}, bf16[80,2048]{1,0:T(8,128)(2,1)}, bf16[256,640]{1,0:T(8,128)(2,1)}) async-done(((bf16[80,1024]{1,0:T(8,128)(2,1)}, bf16[128,640]{1,0:T(8,128)(2,1)}, bf16[80,2048]{1,0:T(8,128)(2,1)}, bf16[80,2048]{1,0:T(8,128)(2,1)}, bf16[256,640]{1,0:T(8,128)(2,1)}), ...) | async-done | bytes 1310736 | tf_op jit(solution)/shard_map/psum | solution.py:311
  (443 shorter events, 218.0 us)
Async XLA Ops:
  7.2 5.3 copy-start.65
  7.2 5.6 copy-start.66
  7.2 5.8 copy-start.67
  7.2 6.1 copy-start.68
  7.2 6.3 copy-start.69
  7.2 6.5 copy-start.70
  7.2 22.6 %copy-start.42 = (bf16[80,256]{1,0:T(8,128)(2,1)S(1)}, bf16[80,256]{1,0:T(8,128)(2,1)}, u32[]{:S(2)}) copy-start(bf16[80,256]{1,0:T(8,128)(2,1)} %param.21) | copy-start | bytes 122884
  7.3 50.7 %all-gather.8.cloned.1.call-start = ((), (), s32[]{:S(2)}) async-start(), calls=%async_computation.13 | async-start | bytes 1474560 | tf_op jit(solution)/shard_map/all_gather | solution.py:146
  8.0 68.0 %all-gather.10.cloned.1.call-start = ((), (), s32[]{:S(2)}) async-start(), calls=%async_computation.14 | async-start | bytes 1638400 | tf_op jit(solution)/shard_map/all_gather | solution.py:194
  29.8 28.1 %copy-start.48 = (f32[640]{0:T(1024)}, f32[640]{0:T(1024)S(1)}, u32[]{:S(2)}) copy-start(f32[640]{0:T(1024)S(1)} %convert_element_type.223) | copy-start | bytes 7684
  29.8 10.3 %copy-start.55 = (f32[256]{0:T(256)}, f32[256]{0:T(256)S(1)}, u32[]{:S(2)}) copy-start(f32[256]{0:T(256)S(1)} %convert_element_type.228) | copy-start | bytes 3076
  39.5 18.4 %copy-start.50 = (f32[640]{0:T(1024)}, f32[640]{0:T(1024)S(1)}, u32[]{:S(2)}) copy-start(f32[640]{0:T(1024)S(1)} %fusion.76) | copy-start | bytes 7684
  43.3 84.3 %all-gather.12.cloned.1.call-start = ((), (), s32[]{:S(2)}) async-start(), calls=%async_computation.15 | async-start | bytes 1638400 | tf_op jit(solution)/shard_map/all_gather | solution.py:195
  55.0 153.8 %all-gather.14.cloned.1.call-start = ((), (), s32[]{:S(2)}) async-start(), calls=%async_computation.16 | async-start | bytes 1474560 | tf_op jit(solution)/shard_map/all_gather | solution.py:149
  55.5 158.5 %all-gather.16.cloned.1.call-start = ((), (), s32[]{:S(2)}) async-start(), calls=%async_computation.17 | async-start | bytes 2949120 | tf_op jit(solution)/shard_map/all_gather | solution.py:150
  56.1 11.2 %copy-start.57 = (f32[256]{0:T(256)}, f32[256]{0:T(256)S(1)}, u32[]{:S(2)}) copy-start(f32[256]{0:T(256)S(1)} %convert_element_type.225) | copy-start | bytes 3076
  60.6 6.8 copy-start.5
  70.6 57.8 %all-to-all-start = ((bf16[640,4,256]{2,0,1:T(8,128)(2,1)}), bf16[640,4,256]{2,0,1:T(8,128)(2,1)}, u32[]{:S(2)}, u32[]{:S(2)}) async-start(bf16[640,4,256]{2,0,1:T(8,128)(2,1)} %pad_maximum_fusion), calls=%async_computation | async-start | bytes 2621440 | tf_op jit(solution)/shard_map/all_to_all | solution.py:197
  75.4 145.2 %all-gather.18.cloned.1.call-start = ((), (), s32[]{:S(2)}) async-start(), calls=%async_computation.18 | async-start | bytes 2949120 | tf_op jit(solution)/shard_map/all_gather | solution.py:151
  167.7 34.8 %all-to-all-start.1 = ((bf16[4,2,81920]{2,1,0:T(2,128)(2,1)}), bf16[4,2,81920]{2,1,0:T(2,128)(2,1)S(1)}, u32[]{:S(2)}, u32[]{:S(2)}) async-start(bf16[4,2,81920]{2,1,0:T(2,128)(2,1)} %reshape.447), calls=%async_computation.1 | async-start | bytes 2621440 | tf_op jit(solution)/shard_map/all_to_all | solution.py:199
  171.3 77.8 %all-gather.20.cloned.1.call-start = ((), (), s32[]{:S(2)}) async-start(), calls=%async_computation.19 | async-start | bytes 2949120 | tf_op jit(solution)/shard_map/all_gather | solution.py:152
  249.1 7.8 copy-start.73
  256.9 8.1 copy-start.29
  258.6 6.5 copy-start.21
  280.0 36.5 %all-to-all-start.2 = ((bf16[4,640,1,256]{3,1,2,0:T(8,128)(2,1)}), bf16[4,640,1,256]{3,1,2,0:T(8,128)(2,1)}, u32[]{:S(2)}, u32[]{:S(2)}) async-start(bf16[4,640,1,256]{3,1,2,0:T(8,128)(2,1)} %pad_maximum_fusion.1), calls=%async_computation.2 | async-start | bytes 2621440 | tf_op jit(solution)/shard_map/all_to_all | solution.py:14
  284.6 203.8 %reduce-scatter.28.cloned.1.call-start = ((), (), s32[]{:S(2)}) async-start(), calls=%async_computation.28 | async-start | bytes 1638400
  352.4 5.1 slice-start
  379.6 5.1 slice-start
  458.8 61.9 %reduce-scatter.12.cloned.1.call-start = ((), (), s32[]{:S(2)}) async-start(), calls=%async_computation.20 | async-start | bytes 1638400 | tf_op jit(solution)/shard_map/reduce_scatter | solution.py:266
  460.1 29.4 %copy-start.45 = (f32[640]{0:T(1024)S(1)}, f32[640]{0:T(1024)}, u32[]{:S(2)}) copy-start(f32[640]{0:T(1024)} %copy-done.44) | copy-start | bytes 7684
  460.1 29.5 %copy-start.60 = (f32[128]{0:T(128)S(1)}, f32[128]{0:T(128)}, u32[]{:S(2)}) copy-start(f32[128]{0:T(128)} %copy-done.59) | copy-start | bytes 1540
  460.2 30.9 %copy-start.12 = (f32[640,256]{0,1:T(8,128)S(1)}, f32[640,256]{0,1:T(8,128)}, u32[]{:S(2)}) copy-start(f32[640,256]{0,1:T(8,128)} %copy-done.11) | copy-start | bytes 1966084
  460.2 30.9 %copy-start.41 = (f32[640]{0:T(1024)S(1)}, f32[640]{0:T(1024)}, u32[]{:S(2)}) copy-start(f32[640]{0:T(1024)} %copy-done.40) | copy-start | bytes 7684
  460.2 30.9 %copy-start.56 = (f32[256]{0:T(256)S(1)}, f32[256]{0:T(256)}, u32[]{:S(2)}) copy-start(f32[256]{0:T(256)} %copy-done.55) | copy-start | bytes 3076
  460.2 169.8 %reduce-scatter.16.cloned.1.call-start = ((), (), s32[]{:S(2)}) async-start(), calls=%async_computation.22 | async-start | bytes 737280 | tf_op jit(solution)/shard_map/reduce_scatter | solution.py:297
  493.5 29.6 %copy-start.28 = (bf16[640,4,1,256]{0,3,1,2:T(8,128)(2,1)S(1)}, bf16[640,4,1,256]{0,3,1,2:T(8,128)(2,1)}, u32[]{:S(2)}) copy-start(bf16[640,4,1,256]{0,3,1,2:T(8,128)(2,1)} %copy.188) | copy-start | bytes 3932164
  493.5 29.6 %copy-start.32 = (bf16[640,640]{0,1:T(8,128)(2,1)S(1)}, bf16[640,640]{0,1:T(8,128)(2,1)}, u32[]{:S(2)}) copy-start(bf16[640,640]{0,1:T(8,128)(2,1)} %copy-done.31) | copy-start | bytes 2457604
  493.6 137.9 %reduce-scatter.18.cloned.1.call-start = ((), (), s32[]{:S(2)}) async-start(), calls=%async_computation.23 | async-start | bytes 737280 | tf_op jit(solution)/shard_map/reduce_scatter | solution.py:298
  523.0 119.8 %reduce-scatter.20.cloned.1.call-start = ((), (), s32[]{:S(2)}) async-start(), calls=%async_computation.24 | async-start | bytes 2949120 | tf_op jit(solution)/shard_map/reduce_scatter | solution.py:299
  526.0 163.8 %reduce-scatter.14.cloned.1.call-start = ((), (), s32[]{:S(2)}) async-start(), calls=%async_computation.21 | async-start | bytes 2949120 | tf_op jit(solution)/shard_map/reduce_scatter | solution.py:296
  575.7 173.9 %reduce-scatter.22.cloned.1.call-start = ((), (), s32[]{:S(2)}) async-start(), calls=%async_computation.25 | async-start | bytes 5898240 | tf_op jit(solution)/shard_map/reduce_scatter | solution.py:300
  583.1 226.7 %reduce-scatter.24.cloned.1.call-start = ((), (), s32[]{:S(2)}) async-start(), calls=%async_computation.26 | async-start | bytes 5898240 | tf_op jit(solution)/shard_map/reduce_scatter | solution.py:301
  589.5 280.1 %reduce-scatter.26.cloned.1.call-start = ((), (), s32[]{:S(2)}) async-start(), calls=%async_computation.27 | async-start | bytes 5898240 | tf_op jit(solution)/shard_map/reduce_scatter | solution.py:302
  597.3 311.2 %all-reduce.23.cloned.1.call-start = ((), (), s32[]{:S(2)}) async-start(), calls=%async_computation.29 | async-start | bytes 169984 | tf_op jit(solution)/shard_map/psum | solution.py:312
  633.0 341.4 %all-reduce.25.cloned.1.call-start = ((), (), s32[]{:S(2)}) async-start(), calls=%async_computation.30 | async-start | bytes 2621440 | tf_op jit(solution)/shard_map/psum | solution.py:311
  751.4 120.1 %copy-start.15 = (bf16[640,640]{0,1:T(8,128)(2,1)S(1)}, bf16[640,640]{0,1:T(8,128)(2,1)}, u32[]{:S(2)}) copy-start(bf16[640,640]{0,1:T(8,128)(2,1)} %get-tuple-element.454) | copy-start | bytes 2457604
  974.4 5.3 copy-start.35
  974.4 6.1 copy-start.34
  (73 other events, 186.5 us)
Sparse Core Ops, SparseCore 0:
  10.0 28.3 all-gather.7
  43.4 32.5 all-gather.9
  78.2 49.3 all-gather.11
  129.3 23.8 all-gather.13
  155.0 30.1 all-gather.15
  186.9 30.1 all-gather.17
  218.9 30.1 all-gather.19
  459.0 29.3 reduce-scatter.27
  490.6 30.0 reduce-scatter.11
  524.3 33.3 reduce-scatter.15
  561.3 34.5 reduce-scatter.17
  599.1 43.6 reduce-scatter.19
  646.1 43.5 reduce-scatter.13
  693.0 56.5 reduce-scatter.21
  753.2 56.5 reduce-scatter.23
  813.0 56.5 reduce-scatter.25
  873.8 34.6 all-reduce.22
  912.2 62.2 all-reduce.24
